TPU v7x, 32 devices: a whole 2x2x4 slice. The times are simulated.
32 devices in a mesh: ctx: 8 (over y, x, core), tp: 4 (over z).
Axes of the slice: x: 2, y: 2, z: 4, core: 2. Of those that a mesh axis runs over, the one named last changes fastest.
Arguments:
- tokens: bfloat16 [8, 1024, 768], P(None, 'ctx'), may hold values from -6 to 6
- cotangent: bfloat16 [8, 1024, 768], P(None, 'ctx'), may hold values from -1.5 to 1.5
- seq_lengths: int32 [8], replicated, may hold values from 256 to 1024, as said below
- combined_weight: bfloat16 [2, 768, 12, 3, 64], P(None, None, 'tp'), may hold values from -0.21875 to 0.21875
- joined_bias: bfloat16 [2, 12, 2, 64], P(None, 'tp'), may hold values from -3 to 3
- attention_out_weight: bfloat16 [2, 768, 768], P(None, 'tp'), may hold values from -9 to 9
- attention_out_bias: bfloat16 [2, 768], replicated, may hold values from -3 to 3
- expand_weight: bfloat16 [2, 768, 3072], P(None, None, 'tp'), may hold values from -0.21875 to 0.21875
- expand_bias: bfloat16 [2, 3072], P(None, 'tp'), may hold values from -3 to 3
- contract_weight: bfloat16 [2, 3072, 768], P(None, 'tp'), may hold values from -0.109375 to 0.109375
- contract_bias: bfloat16 [2, 768], replicated, may hold values from -3 to 3
- norm_gains: bfloat16 [2, 2, 768], replicated, may hold values from 0.25 to 1.75
- norm_shifts: bfloat16 [2, 2, 768], replicated, may hold values from -3 to 3
Outputs:
- outputs: float32 [8, 1024, 768], P(None, 'ctx')
- tokens_grad: float32 [8, 1024, 768], P(None, 'ctx')
- grad_joined: float32 [2, 768, 12, 3, 64], P(None, None, 'tp')
- grad_qvbias: float32 [2, 12, 2, 64], P(None, 'tp')
- grad_mixer: float32 [2, 768, 768], P(None, 'tp')
- grad_mbias: float32 [2, 768], replicated
- grad_upward: float32 [2, 768, 3072], P(None, None, 'tp')
- grad_ubias: float32 [2, 3072], P(None, 'tp')
- grad_down: float32 [2, 3072, 768], P(None, 'tp')
- grad_dbias: float32 [2, 768], replicated
- grad_gains: float32 [2, 2, 768], replicated
- grad_shifts: float32 [2, 2, 768], replicated
Inputs may be any that keep to these rules, and one draw needn't show every extreme that they name: `seq_lengths`: at least one sequence has length 1024 in every draw.
All inputs are finite; a program needn't handle non-finite values.
Results may differ from a plain program's by a relative error of at most 0.018.
Values may be sent and summed in bfloat16 or wider, within the bound.
A program may use at most 448 MiB of HBM per device.

v0:
```python
import jax
import jax.numpy as jnp
from jax import lax
from jax.sharding import PartitionSpec as P

EPS = 1e-12
MASKED = -1e30


def normalize(resid, norm_gain, norm_shift):
    row_mean = jnp.mean(resid, axis=-1, keepdims=True)
    centred = resid - row_mean
    spread = jnp.mean(centred * centred, axis=-1, keepdims=True)
    return centred * lax.rsqrt(spread + EPS) * norm_gain + norm_shift


def smooth_gate(value):
    return (
        0.5
        * value
        * (1.0 + jnp.tanh(0.7978845608028654 * (value + 0.044715 * value * value * value)))
    )


def attention_scores(queries, key_rows, key_valid, scale):
    scores = (
        jnp.einsum("sqhd,skhd->shqk", queries, key_rows, preferred_element_type=jnp.float32) * scale
    )
    return jnp.where(key_valid[:, None, None, :], scores, MASKED)


def share_sum(partial_rows):
    return lax.psum_scatter(partial_rows, "tp", scatter_dimension=1, tiled=True)


def share_gather(rows_low):
    return lax.all_gather(rows_low, "tp", axis=1, tiled=True)


def take_share(full_rows):
    share_rows = full_rows.shape[1] // lax.axis_size("tp")
    return lax.dynamic_slice_in_dim(full_rows, lax.axis_index("tp") * share_rows, share_rows, 1)


def forward_layer(
    hidden,
    hidden_reduced,
    seq_lengths,
    combined_weight,
    joined_bias,
    attention_out_weight,
    attention_out_bias,
    expand_weight,
    expand_bias,
    contract_weight,
    contract_bias,
    norm_gains,
    norm_shifts,
):
    n_seqs, n_rows, width = hidden_reduced.shape
    n_heads = combined_weight.shape[1]
    head_dim = combined_weight.shape[3]
    scale = head_dim ** (-0.5)
    joined_flat = combined_weight.reshape(width, -1)
    combined_projected = jnp.einsum(
        "sbd,dc->sbc", hidden_reduced, joined_flat, preferred_element_type=jnp.float32
    )
    combined_projected = combined_projected.reshape(n_seqs, n_rows, n_heads, 3, head_dim)
    queries = (combined_projected[..., 0, :] + joined_bias[:, 0, :]).astype(jnp.bfloat16)
    key_rows = combined_projected[..., 1, :].astype(jnp.bfloat16)
    value_rows = (combined_projected[..., 2, :] + joined_bias[:, 1, :]).astype(jnp.bfloat16)
    all_keys, all_values = (
        lax.all_gather(key_rows.reshape(n_seqs, n_rows, -1), "ctx", axis=1, tiled=True),
        lax.all_gather(value_rows.reshape(n_seqs, n_rows, -1), "ctx", axis=1, tiled=True),
    )
    total_len = all_keys.shape[1]
    all_keys = all_keys.reshape(n_seqs, total_len, n_heads, head_dim)
    all_values = all_values.reshape(n_seqs, total_len, n_heads, head_dim)
    key_valid = jnp.arange(total_len)[None, :] < seq_lengths[:, None]
    scores = attention_scores(queries, all_keys, key_valid, scale)
    row_max = jnp.max(scores, axis=-1, keepdims=True)
    log_total = row_max + jnp.log(jnp.sum(jnp.exp(scores - row_max), axis=-1, keepdims=True))
    attn_probs = jnp.exp(scores - log_total).astype(jnp.bfloat16)
    merged_head_output = jnp.einsum(
        "shqk,skhd->sqhd", attn_probs, all_values, preferred_element_type=jnp.float32
    )
    merged_head_output = merged_head_output.astype(jnp.bfloat16).reshape(n_seqs, n_rows, -1)
    attention_branch = jnp.einsum(
        "sbc,cd->sbd", merged_head_output, attention_out_weight, preferred_element_type=jnp.float32
    )
    attention_branch = share_sum(attention_branch)
    normalized_rows, first_back = jax.vjp(
        normalize, hidden + attention_branch + attention_out_bias, norm_gains[0], norm_shifts[0]
    )
    normed_low = normalized_rows.astype(jnp.bfloat16)
    normed_low = share_gather(normed_low)
    before_activation = (
        jnp.einsum("sbd,df->sbf", normed_low, expand_weight, preferred_element_type=jnp.float32)
        + expand_bias
    )
    activated_hidden, gate_back = jax.vjp(smooth_gate, before_activation)
    gated_low = activated_hidden.astype(jnp.bfloat16)
    feedforward_branch = jnp.einsum(
        "sbf,fd->sbd", gated_low, contract_weight, preferred_element_type=jnp.float32
    )
    feedforward_branch = share_sum(feedforward_branch)
    result, second_back = jax.vjp(
        normalize,
        normalized_rows + feedforward_branch + contract_bias,
        norm_gains[1],
        norm_shifts[1],
    )
    kept = (
        hidden_reduced,
        queries,
        key_rows,
        value_rows,
        all_keys,
        all_values,
        key_valid,
        log_total,
        merged_head_output,
        normed_low,
        gated_low,
        first_back,
        gate_back,
        second_back,
    )
    return (result, kept)


def backward_layer(
    grad_out, kept, combined_weight, attention_out_weight, expand_weight, contract_weight
):
    (
        hidden_reduced,
        queries,
        key_rows,
        value_rows,
        all_keys,
        all_values,
        key_valid,
        log_total,
        merged_head_output,
        normed_low,
        gated_low,
        first_back,
        gate_back,
        second_back,
    ) = kept
    n_seqs, n_rows, n_heads, head_dim = queries.shape
    width = hidden_reduced.shape[2]
    total_len = all_keys.shape[1]
    scale = head_dim ** (-0.5)
    d_resid_two, d_gain_two, d_shift_two = second_back(grad_out)
    d_down_bias = jnp.sum(d_resid_two, axis=(0, 1))
    d_branch_two = d_resid_two.astype(jnp.bfloat16)
    d_branch_two = share_gather(d_branch_two)
    d_down = jnp.einsum("sbf,sbd->fd", gated_low, d_branch_two, preferred_element_type=jnp.float32)
    d_gated = jnp.einsum(
        "sbd,fd->sbf", d_branch_two, contract_weight, preferred_element_type=jnp.float32
    )
    d_pre_gate = gate_back(d_gated)[0].astype(jnp.bfloat16)
    d_up_bias = jnp.sum(d_pre_gate.astype(jnp.float32), axis=(0, 1))
    d_upward = jnp.einsum("sbd,sbf->df", normed_low, d_pre_gate, preferred_element_type=jnp.float32)
    d_normed = jnp.einsum(
        "sbf,df->sbd", d_pre_gate, expand_weight, preferred_element_type=jnp.float32
    )
    d_normed = share_sum(d_normed) + d_resid_two
    d_resid_one, d_gain_one, d_shift_one = first_back(d_normed)
    d_mixer_bias = jnp.sum(d_resid_one, axis=(0, 1))
    d_branch = d_resid_one.astype(jnp.bfloat16)
    d_branch = share_gather(d_branch)
    d_mixer = jnp.einsum(
        "sbc,sbd->cd", merged_head_output, d_branch, preferred_element_type=jnp.float32
    )
    d_mixed = jnp.einsum(
        "sbd,cd->sbc", d_branch, attention_out_weight, preferred_element_type=jnp.float32
    )
    d_mixed = d_mixed.astype(jnp.bfloat16).reshape(n_seqs, n_rows, n_heads, head_dim)
    scores = attention_scores(queries, all_keys, key_valid, scale)
    probs_full = jnp.exp(scores - log_total)
    d_probs = jnp.einsum("sqhd,skhd->shqk", d_mixed, all_values, preferred_element_type=jnp.float32)
    row_delta = jnp.sum(probs_full * d_probs, axis=-1, keepdims=True)
    d_scores = (probs_full * (d_probs - row_delta)).astype(jnp.bfloat16)
    d_queries = (
        jnp.einsum("shqk,skhd->sqhd", d_scores, all_keys, preferred_element_type=jnp.float32)
        * scale
    )
    d_queries = d_queries.astype(jnp.bfloat16)
    key_part = (
        jnp.einsum("shqk,sqhd->skhd", d_scores, queries, preferred_element_type=jnp.float32) * scale
    )
    value_part = jnp.einsum(
        "shqk,sqhd->skhd",
        probs_full.astype(jnp.bfloat16),
        d_mixed,
        preferred_element_type=jnp.float32,
    )
    d_keys, d_values = (
        lax.psum_scatter(
            key_part.reshape(n_seqs, total_len, -1), "ctx", scatter_dimension=1, tiled=True
        ),
        lax.psum_scatter(
            value_part.reshape(n_seqs, total_len, -1), "ctx", scatter_dimension=1, tiled=True
        ),
    )
    d_keys = d_keys.reshape(n_seqs, n_rows, n_heads, head_dim)
    d_values = d_values.reshape(n_seqs, n_rows, n_heads, head_dim)
    d_keys = d_keys.astype(jnp.bfloat16)
    d_values = d_values.astype(jnp.bfloat16)
    d_joined_bias = jnp.stack(
        [
            jnp.sum(d_queries.astype(jnp.float32), axis=(0, 1)),
            jnp.sum(d_values.astype(jnp.float32), axis=(0, 1)),
        ],
        axis=1,
    )
    d_joined_out = jnp.stack([d_queries, d_keys, d_values], axis=3).reshape(n_seqs, n_rows, -1)
    d_joined = jnp.einsum(
        "sbd,sbc->dc", hidden_reduced, d_joined_out, preferred_element_type=jnp.float32
    )
    d_joined = d_joined.reshape(width, n_heads, 3, head_dim)
    d_hidden = jnp.einsum(
        "sbc,dc->sbd",
        d_joined_out,
        combined_weight.reshape(width, -1),
        preferred_element_type=jnp.float32,
    )
    d_hidden = share_sum(d_hidden) + d_resid_one
    small_grads = (
        d_mixer_bias,
        d_down_bias,
        jnp.stack([d_gain_one, d_gain_two]),
        jnp.stack([d_shift_one, d_shift_two]),
    )
    small_grads = lax.psum(
        (
            small_grads[0],
            small_grads[1],
            small_grads[2].astype(jnp.float32),
            small_grads[3].astype(jnp.float32),
        ),
        "tp",
    )
    grads = (
        d_joined,
        d_joined_bias,
        d_mixer,
        small_grads[0],
        d_upward,
        d_up_bias,
        d_down,
        small_grads[1],
        small_grads[2],
        small_grads[3],
    )
    return (d_hidden, grads)


def sum_layer(grads):
    return lax.psum(
        (
            grads[0],
            grads[1],
            grads[2],
            grads[3],
            grads[4],
            grads[5],
            grads[6],
            grads[7],
            grads[8],
            grads[9],
        ),
        "ctx",
    )


def on_device(
    tokens,
    cotangent,
    seq_lengths,
    combined_weight,
    joined_bias,
    attention_out_weight,
    attention_out_bias,
    expand_weight,
    expand_bias,
    contract_weight,
    contract_bias,
    norm_gains,
    norm_shifts,
):
    params = (
        combined_weight,
        joined_bias,
        attention_out_weight,
        attention_out_bias,
        expand_weight,
        expand_bias,
        contract_weight,
        contract_bias,
        norm_gains,
        norm_shifts,
    )
    n_layers = combined_weight.shape[0]
    hidden = tokens.astype(jnp.float32)
    hidden_reduced = tokens
    hidden = take_share(hidden)
    saved = []
    for layer_idx in range(n_layers):
        hidden, kept = forward_layer(
            hidden, hidden_reduced, seq_lengths, *[weight[layer_idx] for weight in params]
        )
        saved.append(kept)
        if layer_idx + 1 < n_layers:
            hidden_reduced = hidden.astype(jnp.bfloat16)
            hidden_reduced = share_gather(hidden_reduced)
    grad_now = cotangent.astype(jnp.float32)
    grad_now = take_share(grad_now)
    collected = []
    for layer_idx in reversed(range(n_layers)):
        grad_now, grads = backward_layer(
            grad_now,
            saved[layer_idx],
            combined_weight[layer_idx],
            attention_out_weight[layer_idx],
            expand_weight[layer_idx],
            contract_weight[layer_idx],
        )
        grads = sum_layer(grads)
        collected.insert(0, grads)
    stacked = tuple((jnp.stack([entry[member] for entry in collected]) for member in range(10)))
    hidden, grad_now = (
        lax.all_gather(hidden, "tp", axis=1, tiled=True),
        lax.all_gather(grad_now, "tp", axis=1, tiled=True),
    )
    return (
        hidden,
        grad_now,
        stacked[0],
        stacked[1],
        stacked[2],
        stacked[3],
        stacked[4],
        stacked[5],
        stacked[6],
        stacked[7],
        stacked[8],
        stacked[9],
    )


def solution(mesh):
    placed = (
        P(None, "ctx", None),
        P(None, "ctx", None),
        P(),
        P(None, None, "tp", None, None),
        P(None, "tp", None, None),
        P(None, "tp", None),
        P(),
        P(None, None, "tp"),
        P(None, "tp"),
        P(None, "tp", None),
        P(),
        P(),
        P(),
    )
    return jax.shard_map(
        on_device,
        mesh=mesh,
        in_specs=placed,
        out_specs=(
            P(None, "ctx", None),
            P(None, "ctx", None),
            P(None, None, "tp", None, None),
            P(None, "tp", None, None),
            P(None, "tp", None),
            P(),
            P(None, None, "tp"),
            P(None, "tp"),
            P(None, "tp", None),
            P(),
            P(),
            P(),
        ),
        check_vma=False,
    )
```

profile of v0, /device:TPU:0, one launch (start us, length us, event | category | flops | bytes accessed | tf_op | source)
XLA Modules:
  0.0 1609.7 jit_solution(18268180588646631589)
XLA Ops:
  12.3 34.3 %all-gather.16.cloned.1.call-done = bf16[8,1024,192]{1,2,0:T(8,128)(2,1)} async-done(((bf16[8,128,192]{1,2,0:T(8,128)(2,1)}), bf16[8,1024,192]{1,2,0:T(8,128)(2,1)}) %all-gather.16.cloned.1.call-update) | async-done | bytes 3145744 | tf_op jit(solution)/shard_map/all_gather | solution.py:73
  55.1 26.9 %all-gather.14.cloned.1.call-done = bf16[8,1024,192]{1,2,0:T(8,128)(2,1)} async-done(((bf16[8,128,192]{1,2,0:T(8,128)(2,1)}), bf16[8,1024,192]{1,2,0:T(8,128)(2,1)}) %all-gather.14.cloned.1.call-update) | async-done | bytes 3145744 | tf_op jit(solution)/shard_map/all_gather | solution.py:74
  81.9 8.5 convolution_convert_fusion.3
  93.7 60.2 %reduce-scatter.13.cloned.1.call-done = f32[8,32,768]{2,1,0:T(8,128)} async-done(((f32[8,128,768]{2,1,0:T(8,128)}), f32[8,32,768]{2,1,0:T(8,128)}) %reduce-scatter.13.cloned.1.call-update) | async-done | bytes 786448 | tf_op jit(solution)/shard_map/reduce_scatter | solution.py:33
  156.7 37.2 %all-gather.18.cloned.1.call-done = bf16[8,128,768]{2,1,0:T(8,128)(2,1)} async-done(((bf16[8,32,768]{2,1,0:T(8,128)(2,1)}), bf16[8,128,768]{2,1,0:T(8,128)(2,1)}) %all-gather.18.cloned.1.call-update) | async-done | bytes 1572880 | tf_op jit(solution)/shard_map/all_gather | solution.py:37
  203.3 58.6 %reduce-scatter.15.cloned.1.call-done = f32[8,32,768]{2,1,0:T(8,128)} async-done(((f32[8,128,768]{2,1,0:T(8,128)}), f32[8,32,768]{2,1,0:T(8,128)}) %reduce-scatter.15.cloned.1.call-update) | async-done | bytes 786448 | tf_op jit(solution)/shard_map/reduce_scatter | solution.py:33
  265.2 36.7 %all-gather.20.cloned.1.call-done = bf16[8,128,768]{2,1,0:T(8,128)(2,1)} async-done(((bf16[8,32,768]{2,1,0:T(8,128)(2,1)}), bf16[8,128,768]{2,1,0:T(8,128)(2,1)}) %all-gather.20.cloned.1.call-update) | async-done | bytes 1572880 | tf_op jit(solution)/shard_map/all_gather | solution.py:37
  309.3 29.5 %all-gather.24.cloned.1.call-done = bf16[8,1024,192]{1,2,0:T(8,128)(2,1)} async-done(((bf16[8,128,192]{1,2,0:T(8,128)(2,1)}), bf16[8,1024,192]{1,2,0:T(8,128)(2,1)}) %all-gather.24.cloned.1.call-update) | async-done | bytes 3145744 | tf_op jit(solution)/shard_map/all_gather | solution.py:73
  347.5 26.6 %all-gather.22.cloned.1.call-done = bf16[8,1024,192]{1,2,0:T(8,128)(2,1)} async-done(((bf16[8,128,192]{1,2,0:T(8,128)(2,1)}), bf16[8,1024,192]{1,2,0:T(8,128)(2,1)}) %all-gather.22.cloned.1.call-update) | async-done | bytes 3145744 | tf_op jit(solution)/shard_map/all_gather | solution.py:74
  384.9 60.3 %reduce-scatter.17.cloned.1.call-done = f32[8,32,768]{2,1,0:T(8,128)} async-done(((f32[8,128,768]{2,1,0:T(8,128)}), f32[8,32,768]{2,1,0:T(8,128)}) %reduce-scatter.17.cloned.1.call-update) | async-done | bytes 786448 | tf_op jit(solution)/shard_map/reduce_scatter | solution.py:33
  448.1 37.2 %all-gather.26.cloned.1.call-done = bf16[8,128,768]{2,1,0:T(8,128)(2,1)} async-done(((bf16[8,32,768]{2,1,0:T(8,128)(2,1)}), bf16[8,128,768]{2,1,0:T(8,128)(2,1)}) %all-gather.26.cloned.1.call-update) | async-done | bytes 1572880 | tf_op jit(solution)/shard_map/all_gather | solution.py:37
  494.3 59.1 %reduce-scatter.19.cloned.1.call-done = f32[8,32,768]{2,1,0:T(8,128)} async-done(((f32[8,128,768]{2,1,0:T(8,128)}), f32[8,32,768]{2,1,0:T(8,128)}) %reduce-scatter.19.cloned.1.call-update) | async-done | bytes 786448 | tf_op jit(solution)/shard_map/reduce_scatter | solution.py:33
  558.8 37.2 %all-gather.30.cloned.1.call-done = bf16[8,128,768]{2,1,0:T(8,128)(2,1)} async-done(((bf16[8,32,768]{2,1,0:T(8,128)(2,1)}), bf16[8,128,768]{2,1,0:T(8,128)(2,1)}) %all-gather.30.cloned.1.call-update) | async-done | bytes 1572880 | tf_op jit(solution)/shard_map/all_gather | solution.py:37
  607.4 59.2 %reduce-scatter.21.cloned.1.call-done = f32[8,32,768]{2,1,0:T(8,128)} async-done(((f32[8,128,768]{2,1,0:T(8,128)}), f32[8,32,768]{2,1,0:T(8,128)}) %reduce-scatter.21.cloned.1.call-update) | async-done | bytes 786448 | tf_op jit(solution)/shard_map/reduce_scatter | solution.py:33
  671.0 37.2 %all-gather.32.cloned.1.call-done = bf16[8,128,768]{2,1,0:T(8,128)(2,1)} async-done(((bf16[8,32,768]{2,1,0:T(8,128)(2,1)}), bf16[8,128,768]{2,1,0:T(8,128)(2,1)}) %all-gather.32.cloned.1.call-update) | async-done | bytes 1572880 | tf_op jit(solution)/shard_map/all_gather | solution.py:37
  710.3 10.3 fusion.75
  752.1 29.3 %reduce-scatter.25.cloned.1.call-done = f32[8,128,192]{1,2,0:T(8,128)} async-done(((f32[8,1024,192]{1,2,0:T(8,128)}), f32[8,128,192]{1,2,0:T(8,128)}) %reduce-scatter.25.cloned.1.call-update) | async-done | bytes 786448 | tf_op jit(solution)/shard_map/reduce_scatter | solution.py:204
  783.3 63.5 %reduce-scatter.23.cloned.1.call-done = f32[8,128,192]{1,2,0:T(8,128)} async-done(((f32[8,1024,192]{1,2,0:T(8,128)}), f32[8,128,192]{1,2,0:T(8,128)}) %reduce-scatter.23.cloned.1.call-update) | async-done | bytes 786448 | tf_op jit(solution)/shard_map/reduce_scatter | solution.py:201
  852.5 60.3 %reduce-scatter.27.cloned.1.call-done = f32[8,32,768]{2,1,0:T(8,128)} async-done(((f32[8,128,768]{2,1,0:T(8,128)}), f32[8,32,768]{2,1,0:T(8,128)}) %reduce-scatter.27.cloned.1.call-update) | async-done | bytes 786448 | tf_op jit(solution)/shard_map/reduce_scatter | solution.py:33
  916.6 37.0 %all-gather.34.cloned.1.call-done = bf16[8,128,768]{2,1,0:T(8,128)(2,1)} async-done(((bf16[8,32,768]{2,1,0:T(8,128)(2,1)}), bf16[8,128,768]{2,1,0:T(8,128)(2,1)}) %all-gather.34.cloned.1.call-update) | async-done | bytes 1572880 | tf_op jit(solution)/shard_map/all_gather | solution.py:37
  964.9 59.2 %reduce-scatter.29.cloned.1.call-done = f32[8,32,768]{2,1,0:T(8,128)} async-done(((f32[8,128,768]{2,1,0:T(8,128)}), f32[8,32,768]{2,1,0:T(8,128)}) %reduce-scatter.29.cloned.1.call-update) | async-done | bytes 786448 | tf_op jit(solution)/shard_map/reduce_scatter | solution.py:33
  1029.1 37.2 %all-gather.36.cloned.1.call-done = bf16[8,128,768]{2,1,0:T(8,128)(2,1)} async-done(((bf16[8,32,768]{2,1,0:T(8,128)(2,1)}), bf16[8,128,768]{2,1,0:T(8,128)(2,1)}) %all-gather.36.cloned.1.call-update) | async-done | bytes 1572880 | tf_op jit(solution)/shard_map/all_gather | solution.py:37
  1068.4 10.2 fusion.78
  1080.5 8.9 multiply_reduce_fusion
  1110.1 29.3 %reduce-scatter.33.cloned.1.call-done = f32[8,128,192]{1,2,0:T(8,128)} async-done(((f32[8,1024,192]{1,2,0:T(8,128)}), f32[8,128,192]{1,2,0:T(8,128)}) %reduce-scatter.33.cloned.1.call-update) | async-done | bytes 786448 | tf_op jit(solution)/shard_map/reduce_scatter | solution.py:204
  1140.7 64.2 %reduce-scatter.31.cloned.1.call-done = f32[8,128,192]{1,2,0:T(8,128)} async-done(((f32[8,1024,192]{1,2,0:T(8,128)}), f32[8,128,192]{1,2,0:T(8,128)}) %reduce-scatter.31.cloned.1.call-update) | async-done | bytes 786448 | tf_op jit(solution)/shard_map/reduce_scatter | solution.py:201
  1232.4 37.5 %reduce-scatter.35.cloned.1.call-done = f32[8,32,768]{2,1,0:T(8,128)} async-done(((f32[8,128,768]{2,1,0:T(8,128)}), f32[8,32,768]{2,1,0:T(8,128)}) %reduce-scatter.35.cloned.1.call-update) | async-done | bytes 786448 | tf_op jit(solution)/shard_map/reduce_scatter | solution.py:33
  1272.2 62.7 %all-gather.28.cloned.1.call-done = f32[8,128,768]{2,1,0:T(8,128)} async-done(((f32[8,32,768]{2,1,0:T(8,128)}), f32[8,128,768]{2,1,0:T(8,128)}) %all-gather.28.cloned.1.call-update) | async-done | bytes 3145744 | tf_op jit(solution)/shard_map/all_gather | solution.py:335
  1335.2 16.9 %all-reduce.2 = (f32[768]{0:T(1024)S(1)}, f32[768]{0:T(1024)S(1)}, f32[768]{0:T(1024)S(1)}, f32[768]{0:T(1024)S(1)}, f32[2,768]{1,0:T(2,128)S(1)}, /*index=5*/f3...) all-reduce(f32[768]{0:T(1024)S(1)} %copy-done.53, ...), channel_id=1, replica_groups=mesh['ctx'=8,'tp'=4] {'tp'}, use_global_device_ids=true, to_apply=%region_48.49 | all-reduce | flops 9216 | bytes 73728 | tf_op jit(solution)/shard_map/psum | solution.py:237
  1352.3 25.3 %all-reduce = (f32[1,3,2,64]{3,2,1,0:T(2,128)S(1)}, f32[1,3,2,64]{3,2,1,0:T(2,128)S(1)}, f32[1,768]{1,0:T(1,128)S(1)}, f32[1,768]{1,0:T(1,128)S(1)}, f32[1,768]{...) all-reduce(f32[1,3,2,64]{3,2,1,0:T(2,128)S(1)} %maximum_bitcast_fus, ...), channel_id=1, replica_groups=mesh['ctx'=8,'tp'=4] {'ctx'}, use_global_device_ids=true, to_apply=%region_41.42 | all-reduce | flops 11520 | bytes 92160 | tf_op jit(solution)/shard_map/psum | solution.py:262
  1381.2 151.4 %all-reduce.5.cloned.1.call-done = (f32[1,768,3,3,64]{1,4,3,2,0:T(8,128)}, f32[1,768,3,3,64]{1,4,3,2,0:T(8,128)}, f32[1,192,768]{2,1,0:T(8,128)}, f32[1,192,768]...) async-done(((f32[1,768,3,3,64]{1,4,3,2,0:T(8,128)}, f32[1,768,3,3,64]{1,4,3,2,0:T(8,128)}, ...) | async-done | bytes 14155792 | tf_op jit(solution)/shard_map/psum | solution.py:262
  1545.8 52.5 %all-gather.38.cloned.1.call-done = f32[8,128,768]{2,1,0:T(8,128)} async-done(((f32[8,32,768]{2,1,0:T(8,128)}), f32[8,128,768]{2,1,0:T(8,128)}) %all-gather.38.cloned.1.call-update) | async-done | bytes 3145744 | tf_op jit(solution)/shard_map/all_gather | solution.py:336
  (377 shorter events, 229.5 us)
Async XLA Ops:
  7.2 39.4 %all-gather.16.cloned.1.call-start = ((), (), s32[]{:S(2)}) async-start(), calls=%async_computation.13 | async-start | bytes 3538944 | tf_op jit(solution)/shard_map/all_gather | solution.py:73
  10.9 71.0 %all-gather.14.cloned.1.call-start = ((), (), s32[]{:S(2)}) async-start(), calls=%async_computation.12 | async-start | bytes 3538944 | tf_op jit(solution)/shard_map/all_gather | solution.py:74
  12.1 141.8 %reduce-scatter.13.cloned.1.call-start = ((), (), s32[]{:S(2)}) async-start(), calls=%async_computation.14 | async-start | bytes 3932160 | tf_op jit(solution)/shard_map/reduce_scatter | solution.py:33
  93.5 100.3 %all-gather.18.cloned.1.call-start = ((), (), s32[]{:S(2)}) async-start(), calls=%async_computation.15 | async-start | bytes 1966080 | tf_op jit(solution)/shard_map/all_gather | solution.py:37
  93.7 168.2 %copy-start.33 = (f32[768]{0:T(1024)}, f32[768]{0:T(1024)S(1)}, u32[]{:S(2)}) copy-start(f32[768]{0:T(1024)S(1)} %get-tuple-element.122) | copy-start | bytes 9220
  93.7 351.5 %copy-start.35 = (f32[768]{0:T(1024)}, f32[768]{0:T(1024)S(1)}, u32[]{:S(2)}) copy-start(f32[768]{0:T(1024)S(1)} %get-tuple-element.123) | copy-start | bytes 9220
  155.6 106.3 %copy-start.37 = (f32[8,32]{1,0:T(8,128)}, f32[8,32]{1,0:T(8,128)S(1)}, u32[]{:S(2)}) copy-start(f32[8,32]{1,0:T(8,128)S(1)} %fusion.87) | copy-start | bytes 3076
  156.6 105.3 %reduce-scatter.15.cloned.1.call-start = ((), (), s32[]{:S(2)}) async-start(), calls=%async_computation.16 | async-start | bytes 3932160 | tf_op jit(solution)/shard_map/reduce_scatter | solution.py:33
  156.7 439.4 %copy-start.70 = (f32[768]{0:T(1024)}, f32[768]{0:T(1024)S(1)}, u32[]{:S(2)}) copy-start(f32[768]{0:T(1024)S(1)} %get-tuple-element.36) | copy-start | bytes 9220
  202.6 99.3 %all-gather.20.cloned.1.call-start = ((), (), s32[]{:S(2)}) async-start(), calls=%async_computation.17 | async-start | bytes 1966080 | tf_op jit(solution)/shard_map/all_gather | solution.py:37
  263.7 181.5 %copy-start.39 = (f32[8,32]{1,0:T(8,128)}, f32[8,32]{1,0:T(8,128)S(1)}, u32[]{:S(2)}) copy-start(f32[8,32]{1,0:T(8,128)S(1)} %fusion.88) | copy-start | bytes 3076
  264.7 74.1 %all-gather.24.cloned.1.call-start = ((), (), s32[]{:S(2)}) async-start(), calls=%async_computation.19 | async-start | bytes 3538944 | tf_op jit(solution)/shard_map/all_gather | solution.py:73
  307.0 67.1 %all-gather.22.cloned.1.call-start = ((), (), s32[]{:S(2)}) async-start(), calls=%async_computation.18 | async-start | bytes 3538944 | tf_op jit(solution)/shard_map/all_gather | solution.py:74
  309.2 136.0 %reduce-scatter.17.cloned.1.call-start = ((), (), s32[]{:S(2)}) async-start(), calls=%async_computation.20 | async-start | bytes 3932160 | tf_op jit(solution)/shard_map/reduce_scatter | solution.py:33
  384.9 100.4 %all-gather.26.cloned.1.call-start = ((), (), s32[]{:S(2)}) async-start(), calls=%async_computation.21 | async-start | bytes 1966080 | tf_op jit(solution)/shard_map/all_gather | solution.py:37
  448.0 105.3 %reduce-scatter.19.cloned.1.call-start = ((), (), s32[]{:S(2)}) async-start(), calls=%async_computation.22 | async-start | bytes 3932160 | tf_op jit(solution)/shard_map/reduce_scatter | solution.py:33
  494.0 102.0 %all-gather.30.cloned.1.call-start = ((), (), s32[]{:S(2)}) async-start(), calls=%async_computation.24 | async-start | bytes 1966080 | tf_op jit(solution)/shard_map/all_gather | solution.py:37
  558.8 107.8 %reduce-scatter.21.cloned.1.call-start = ((), (), s32[]{:S(2)}) async-start(), calls=%async_computation.25 | async-start | bytes 3932160 | tf_op jit(solution)/shard_map/reduce_scatter | solution.py:33
  607.3 100.9 %all-gather.32.cloned.1.call-start = ((), (), s32[]{:S(2)}) async-start(), calls=%async_computation.26 | async-start | bytes 1966080 | tf_op jit(solution)/shard_map/all_gather | solution.py:37
  670.9 110.5 %reduce-scatter.25.cloned.1.call-start = ((), (), s32[]{:S(2)}) async-start(), calls=%async_computation.28 | async-start | bytes 7077888 | tf_op jit(solution)/shard_map/reduce_scatter | solution.py:204
  720.6 126.2 %reduce-scatter.23.cloned.1.call-start = ((), (), s32[]{:S(2)}) async-start(), calls=%async_computation.27 | async-start | bytes 7077888 | tf_op jit(solution)/shard_map/reduce_scatter | solution.py:201
  742.7 170.1 %reduce-scatter.27.cloned.1.call-start = ((), (), s32[]{:S(2)}) async-start(), calls=%async_computation.29 | async-start | bytes 3932160 | tf_op jit(solution)/shard_map/reduce_scatter | solution.py:33
  852.4 101.1 %all-gather.34.cloned.1.call-start = ((), (), s32[]{:S(2)}) async-start(), calls=%async_computation.30 | async-start | bytes 1966080 | tf_op jit(solution)/shard_map/all_gather | solution.py:37
  916.3 107.8 %reduce-scatter.29.cloned.1.call-start = ((), (), s32[]{:S(2)}) async-start(), calls=%async_computation.31 | async-start | bytes 3932160 | tf_op jit(solution)/shard_map/reduce_scatter | solution.py:33
  964.9 101.5 %all-gather.36.cloned.1.call-start = ((), (), s32[]{:S(2)}) async-start(), calls=%async_computation.32 | async-start | bytes 1966080 | tf_op jit(solution)/shard_map/all_gather | solution.py:37
  1029.1 110.4 %reduce-scatter.33.cloned.1.call-start = ((), (), s32[]{:S(2)}) async-start(), calls=%async_computation.34 | async-start | bytes 7077888 | tf_op jit(solution)/shard_map/reduce_scatter | solution.py:204
  1078.7 126.3 %reduce-scatter.31.cloned.1.call-start = ((), (), s32[]{:S(2)}) async-start(), calls=%async_computation.33 | async-start | bytes 7077888 | tf_op jit(solution)/shard_map/reduce_scatter | solution.py:201
  1103.1 166.8 %reduce-scatter.35.cloned.1.call-start = ((), (), s32[]{:S(2)}) async-start(), calls=%async_computation.35 | async-start | bytes 3932160 | tf_op jit(solution)/shard_map/reduce_scatter | solution.py:33
  1209.5 125.3 %all-gather.28.cloned.1.call-start = ((), (), s32[]{:S(2)}) async-start(), calls=%async_computation.23 | async-start | bytes 3932160 | tf_op jit(solution)/shard_map/all_gather | solution.py:335
  1210.1 322.5 %all-reduce.5.cloned.1.call-start = ((), (), s32[]{:S(2)}) async-start(), calls=%async_computation.37 | async-start | bytes 28311552 | tf_op jit(solution)/shard_map/psum | solution.py:262
  1232.3 102.9 %copy-start.52 = (f32[768]{0:T(1024)S(1)}, f32[768]{0:T(1024)}, u32[]{:S(2)}) copy-start(f32[768]{0:T(1024)} %get-tuple-element.13) | copy-start | bytes 9220
  1232.4 366.0 %all-gather.38.cloned.1.call-start = ((), (), s32[]{:S(2)}) async-start(), calls=%async_computation.36 | async-start | bytes 3932160 | tf_op jit(solution)/shard_map/all_gather | solution.py:336
  (86 other events, 2623.3 us)
Sparse Core Ops, SparseCore 0:
  11.1 35.5 all-gather.15
  49.1 32.8 all-gather.13
  93.6 60.2 reduce-scatter.12
  156.7 37.1 all-gather.17
  202.7 59.1 reduce-scatter.14
  264.8 37.0 all-gather.19
  307.1 31.6 all-gather.23
  341.2 32.8 all-gather.21
  385.0 60.2 reduce-scatter.16
  448.1 37.1 all-gather.25
  494.2 59.1 reduce-scatter.18
  558.9 37.0 all-gather.29
  607.4 59.0 reduce-scatter.20
  671.1 37.1 all-gather.31
  720.7 60.6 reduce-scatter.24
  785.0 61.7 reduce-scatter.22
  852.6 60.2 reduce-scatter.26
  916.4 37.0 all-gather.33
  965.0 59.0 reduce-scatter.28
  1029.2 37.1 all-gather.35
  1078.8 60.6 reduce-scatter.32
  1143.2 61.7 reduce-scatter.30
  1209.6 60.2 reduce-scatter.34
  1271.4 63.4 all-gather.27
  1340.7 191.8 all-reduce.4
  1534.7 63.5 all-gather.37
where the time goes:
time: 1620 us; the launch traced here: 1610 us
  waiting for transfers between devices  1290 us (80%)
  matrix products  162 us (10%)
  other arithmetic  73.8 us (5%)
  blocking collectives  42.2 us (3%)
  local copies, waits for them, and re-layouts  28.2 us (2%)
    reduce_scatter x8, waiting for transfers between devices, share_sum(): return lax.psum_scatter(partial_rows, 'tp', scatter_dimension=1, tiled=True)  454 us
    all_gather x7, waiting for transfers between devices, share_gather(): return lax.all_gather(rows_low, 'tp', axis=1, tiled=True)  260 us
    psum x1, waiting for transfers between devices, sum_layer(): lax.psum((grads[0], grads[1], grads[2], grads[3], grads[4], grads[5], gra...  151 us
    reduce_scatter x2, waiting for transfers between devices, backward_layer(): lax.psum_scatter(key_part.reshape(n_seqs, total_len, -1), 'ctx', scatter_...  128 us
    all_gather x2, waiting for transfers between devices, forward_layer(): lax.all_gather(key_rows.reshape(n_seqs, n_rows, -1), 'ctx', axis=1, tiled...  63.8 us
    all_gather x1, waiting for transfers between devices, on_device(): lax.all_gather(hidden, 'tp', axis=1, tiled=True)  62.7 us
    reduce_scatter x2, waiting for transfers between devices, backward_layer(): lax.psum_scatter(value_part.reshape(n_seqs, total_len, -1), 'ctx', scatte...  58.6 us
    all_gather x2, waiting for transfers between devices, forward_layer(): lax.all_gather(value_rows.reshape(n_seqs, n_rows, -1), 'ctx', axis=1, til...  53.5 us
  transfers between devices with their start and end apart: 26, of which 26 were waited for; matrix products, arithmetic and copies ran while one was open for 7% of the time, Pallas kernels for 0%

commit v1 on v0

--- a/solution.py
+++ b/solution.py
@@ -5,6 +5,35 @@
 
 EPS = 1e-12
 MASKED = -1e30
+
+
+def _tell_types(q_in, ndim_at):
+    q_in = jnp.moveaxis(q_in, 0, ndim_at)
+    aux = q_in.shape
+    return q_in.reshape(*aux[:ndim_at], aux[ndim_at] * aux[ndim_at + 1], *aux[ndim_at + 2 :])
+
+
+def target_treat(local_values, shard_axis):
+    carry_out = lax.axis_size(shard_axis)
+    h_now = lax.axis_index(shard_axis)
+    right_arr, left_arr = (carry_out, h_now)
+    low, side_arr = (local_values[None], 1)
+    while side_arr < right_arr:
+        piece_next = range(right_arr)
+        long_array = map(lambda dev_j: (dev_j, dev_j ^ side_arr), piece_next)
+        everything = list(long_array)
+        state_now = lax.ppermute(low, shard_axis, everything)
+        heard = left_arr & side_arr == 0
+        after = jnp.where(heard, low, state_now)
+        known = jnp.where(heard, state_now, low)
+        low = jnp.concatenate([after, known])
+        side_arr *= 2
+    return low
+
+
+def _find_case(frame, payload, axis_no):
+    z = target_treat(frame, payload)
+    return _tell_types(z, axis_no)
 
 
 def normalize(resid, norm_gain, norm_shift):
@@ -332,7 +361,7 @@
         collected.insert(0, grads)
     stacked = tuple((jnp.stack([entry[member] for entry in collected]) for member in range(10)))
     hidden, grad_now = (
-        lax.all_gather(hidden, "tp", axis=1, tiled=True),
+        _find_case(hidden, "tp", 1),
         lax.all_gather(grad_now, "tp", axis=1, tiled=True),
     )
     return (

time: 1620 us -> 1570 us (0.969)
  waiting for transfers between devices: 1290 us -> 1230 us
    psum x1, waiting for transfers between devices: 151 us -> 74.9 us  [sum_layer(): lax.psum((grads[0], grads[1], grads[2], grads[3], grads[4], grads[5], gra...]
    ppermute x0 -> x2, waiting for transfers between devices: none -> 68 us  [target_treat(): state_now = lax.ppermute(low, shard_axis, everything)]
    all_gather x1 -> x0, waiting for transfers between devices: 62.7 us -> none  [on_device(): lax.all_gather(hidden, 'tp', axis=1, tiled=True)]
  transfers between devices with their start and end apart: 26 -> 27, of which waited for: 26 -> 26; matrix products, arithmetic and copies ran while one was open for 7% -> 8% of each run, Pallas kernels for 0% -> 0%
where the time goes in v1:
time: 1570 us; the launch traced here: 1560 us
  waiting for transfers between devices  1230 us (78%)
  matrix products  161 us (10%)
  other arithmetic  76.4 us (5%)
  blocking collectives  42 us (3%)
  local copies, waits for them, and re-layouts  31.5 us (2%)
  between operations  15.9 us (1%)
    reduce_scatter x8, waiting for transfers between devices, share_sum(): return lax.psum_scatter(partial_rows, 'tp', scatter_dimension=1, tiled=True)  468 us
    all_gather x7, waiting for transfers between devices, share_gather(): return lax.all_gather(rows_low, 'tp', axis=1, tiled=True)  260 us
    reduce_scatter x2, waiting for transfers between devices, backward_layer(): lax.psum_scatter(key_part.reshape(n_seqs, total_len, -1), 'ctx', scatter_...  127 us
    psum x1, waiting for transfers between devices, sum_layer(): lax.psum((grads[0], grads[1], grads[2], grads[3], grads[4], grads[5], gra...  74.9 us
    ppermute x2, waiting for transfers between devices, target_treat(): state_now = lax.ppermute(low, shard_axis, everything)  68 us
    all_gather x2, waiting for transfers between devices, forward_layer(): lax.all_gather(key_rows.reshape(n_seqs, n_rows, -1), 'ctx', axis=1, tiled...  63.8 us
    reduce_scatter x2, waiting for transfers between devices, backward_layer(): lax.psum_scatter(value_part.reshape(n_seqs, total_len, -1), 'ctx', scatte...  58.5 us
    all_gather x2, waiting for transfers between devices, forward_layer(): lax.all_gather(value_rows.reshape(n_seqs, n_rows, -1), 'ctx', axis=1, til...  53.5 us
  transfers between devices with their start and end apart: 27, of which 26 were waited for; matrix products, arithmetic and copies ran while one was open for 8% of the time, Pallas kernels for 0%

profile of v1, /device:TPU:0, one launch (start us, length us, event | category | flops | bytes accessed | tf_op | source)
XLA Modules:
  0.0 1561.3 jit_solution(11830162962878777209)
XLA Ops:
  12.3 34.3 %all-gather.15.cloned.1.call-done = bf16[8,1024,192]{1,2,0:T(8,128)(2,1)} async-done(((bf16[8,128,192]{1,2,0:T(8,128)(2,1)}), bf16[8,1024,192]{1,2,0:T(8,128)(2,1)}) %all-gather.15.cloned.1.call-update) | async-done | bytes 3145744 | tf_op jit(solution)/shard_map/all_gather | solution.py:102
  55.1 26.9 %all-gather.13.cloned.1.call-done = bf16[8,1024,192]{1,2,0:T(8,128)(2,1)} async-done(((bf16[8,128,192]{1,2,0:T(8,128)(2,1)}), bf16[8,1024,192]{1,2,0:T(8,128)(2,1)}) %all-gather.13.cloned.1.call-update) | async-done | bytes 3145744 | tf_op jit(solution)/shard_map/all_gather | solution.py:103
  81.9 8.5 convolution_convert_fusion.3
  93.7 60.2 %reduce-scatter.13.cloned.1.call-done = f32[8,32,768]{2,1,0:T(8,128)} async-done(((f32[8,128,768]{2,1,0:T(8,128)}), f32[8,32,768]{2,1,0:T(8,128)}) %reduce-scatter.13.cloned.1.call-update) | async-done | bytes 786448 | tf_op jit(solution)/shard_map/reduce_scatter | solution.py:62
  156.7 37.2 %all-gather.17.cloned.1.call-done = bf16[8,128,768]{2,1,0:T(8,128)(2,1)} async-done(((bf16[8,32,768]{2,1,0:T(8,128)(2,1)}), bf16[8,128,768]{2,1,0:T(8,128)(2,1)}) %all-gather.17.cloned.1.call-update) | async-done | bytes 1572880 | tf_op jit(solution)/shard_map/all_gather | solution.py:66
  203.3 58.6 %reduce-scatter.15.cloned.1.call-done = f32[8,32,768]{2,1,0:T(8,128)} async-done(((f32[8,128,768]{2,1,0:T(8,128)}), f32[8,32,768]{2,1,0:T(8,128)}) %reduce-scatter.15.cloned.1.call-update) | async-done | bytes 786448 | tf_op jit(solution)/shard_map/reduce_scatter | solution.py:62
  264.9 37.0 %all-gather.19.cloned.1.call-done = bf16[8,128,768]{2,1,0:T(8,128)(2,1)} async-done(((bf16[8,32,768]{2,1,0:T(8,128)(2,1)}), bf16[8,128,768]{2,1,0:T(8,128)(2,1)}) %all-gather.19.cloned.1.call-update) | async-done | bytes 1572880 | tf_op jit(solution)/shard_map/all_gather | solution.py:66
  309.3 29.5 %all-gather.23.cloned.1.call-done = bf16[8,1024,192]{1,2,0:T(8,128)(2,1)} async-done(((bf16[8,128,192]{1,2,0:T(8,128)(2,1)}), bf16[8,1024,192]{1,2,0:T(8,128)(2,1)}) %all-gather.23.cloned.1.call-update) | async-done | bytes 3145744 | tf_op jit(solution)/shard_map/all_gather | solution.py:102
  347.5 26.6 %all-gather.21.cloned.1.call-done = bf16[8,1024,192]{1,2,0:T(8,128)(2,1)} async-done(((bf16[8,128,192]{1,2,0:T(8,128)(2,1)}), bf16[8,1024,192]{1,2,0:T(8,128)(2,1)}) %all-gather.21.cloned.1.call-update) | async-done | bytes 3145744 | tf_op jit(solution)/shard_map/all_gather | solution.py:103
  384.9 60.3 %reduce-scatter.17.cloned.1.call-done = f32[8,32,768]{2,1,0:T(8,128)} async-done(((f32[8,128,768]{2,1,0:T(8,128)}), f32[8,32,768]{2,1,0:T(8,128)}) %reduce-scatter.17.cloned.1.call-update) | async-done | bytes 786448 | tf_op jit(solution)/shard_map/reduce_scatter | solution.py:62
  448.1 37.2 %all-gather.25.cloned.1.call-done = bf16[8,128,768]{2,1,0:T(8,128)(2,1)} async-done(((bf16[8,32,768]{2,1,0:T(8,128)(2,1)}), bf16[8,128,768]{2,1,0:T(8,128)(2,1)}) %all-gather.25.cloned.1.call-update) | async-done | bytes 1572880 | tf_op jit(solution)/shard_map/all_gather | solution.py:66
  494.3 59.0 %reduce-scatter.19.cloned.1.call-done = f32[8,32,768]{2,1,0:T(8,128)} async-done(((f32[8,128,768]{2,1,0:T(8,128)}), f32[8,32,768]{2,1,0:T(8,128)}) %reduce-scatter.19.cloned.1.call-update) | async-done | bytes 786448 | tf_op jit(solution)/shard_map/reduce_scatter | solution.py:62
  558.8 37.2 %all-gather.27.cloned.1.call-done = bf16[8,128,768]{2,1,0:T(8,128)(2,1)} async-done(((bf16[8,32,768]{2,1,0:T(8,128)(2,1)}), bf16[8,128,768]{2,1,0:T(8,128)(2,1)}) %all-gather.27.cloned.1.call-update) | async-done | bytes 1572880 | tf_op jit(solution)/shard_map/all_gather | solution.py:66
  607.4 59.2 %reduce-scatter.21.cloned.1.call-done = f32[8,32,768]{2,1,0:T(8,128)} async-done(((f32[8,128,768]{2,1,0:T(8,128)}), f32[8,32,768]{2,1,0:T(8,128)}) %reduce-scatter.21.cloned.1.call-update) | async-done | bytes 786448 | tf_op jit(solution)/shard_map/reduce_scatter | solution.py:62
  671.0 37.2 %all-gather.29.cloned.1.call-done = bf16[8,128,768]{2,1,0:T(8,128)(2,1)} async-done(((bf16[8,32,768]{2,1,0:T(8,128)(2,1)}), bf16[8,128,768]{2,1,0:T(8,128)(2,1)}) %all-gather.29.cloned.1.call-update) | async-done | bytes 1572880 | tf_op jit(solution)/shard_map/all_gather | solution.py:66
  710.3 10.3 fusion.75
  752.2 29.2 %reduce-scatter.25.cloned.1.call-done = f32[8,128,192]{1,2,0:T(8,128)} async-done(((f32[8,1024,192]{1,2,0:T(8,128)}), f32[8,128,192]{1,2,0:T(8,128)}) %reduce-scatter.25.cloned.1.call-update) | async-done | bytes 786448 | tf_op jit(solution)/shard_map/reduce_scatter | solution.py:233
  783.3 63.5 %reduce-scatter.23.cloned.1.call-done = f32[8,128,192]{1,2,0:T(8,128)} async-done(((f32[8,1024,192]{1,2,0:T(8,128)}), f32[8,128,192]{1,2,0:T(8,128)}) %reduce-scatter.23.cloned.1.call-update) | async-done | bytes 786448 | tf_op jit(solution)/shard_map/reduce_scatter | solution.py:230
  852.5 60.3 %reduce-scatter.27.cloned.1.call-done = f32[8,32,768]{2,1,0:T(8,128)} async-done(((f32[8,128,768]{2,1,0:T(8,128)}), f32[8,32,768]{2,1,0:T(8,128)}) %reduce-scatter.27.cloned.1.call-update) | async-done | bytes 786448 | tf_op jit(solution)/shard_map/reduce_scatter | solution.py:62
  916.5 37.0 %all-gather.31.cloned.1.call-done = bf16[8,128,768]{2,1,0:T(8,128)(2,1)} async-done(((bf16[8,32,768]{2,1,0:T(8,128)(2,1)}), bf16[8,128,768]{2,1,0:T(8,128)(2,1)}) %all-gather.31.cloned.1.call-update) | async-done | bytes 1572880 | tf_op jit(solution)/shard_map/all_gather | solution.py:66
  964.9 59.2 %reduce-scatter.29.cloned.1.call-done = f32[8,32,768]{2,1,0:T(8,128)} async-done(((f32[8,128,768]{2,1,0:T(8,128)}), f32[8,32,768]{2,1,0:T(8,128)}) %reduce-scatter.29.cloned.1.call-update) | async-done | bytes 786448 | tf_op jit(solution)/shard_map/reduce_scatter | solution.py:62
  1029.1 37.2 %all-gather.33.cloned.1.call-done = bf16[8,128,768]{2,1,0:T(8,128)(2,1)} async-done(((bf16[8,32,768]{2,1,0:T(8,128)(2,1)}), bf16[8,128,768]{2,1,0:T(8,128)(2,1)}) %all-gather.33.cloned.1.call-update) | async-done | bytes 1572880 | tf_op jit(solution)/shard_map/all_gather | solution.py:66
  1068.4 10.2 fusion.78
  1080.5 8.9 multiply_reduce_fusion
  1110.1 29.3 %reduce-scatter.33.cloned.1.call-done = f32[8,128,192]{1,2,0:T(8,128)} async-done(((f32[8,1024,192]{1,2,0:T(8,128)}), f32[8,128,192]{1,2,0:T(8,128)}) %reduce-scatter.33.cloned.1.call-update) | async-done | bytes 786448 | tf_op jit(solution)/shard_map/reduce_scatter | solution.py:233
  1141.3 63.7 %reduce-scatter.31.cloned.1.call-done = f32[8,128,192]{1,2,0:T(8,128)} async-done(((f32[8,1024,192]{1,2,0:T(8,128)}), f32[8,128,192]{1,2,0:T(8,128)}) %reduce-scatter.31.cloned.1.call-update) | async-done | bytes 786448 | tf_op jit(solution)/shard_map/reduce_scatter | solution.py:230
  1235.0 51.5 %reduce-scatter.35.cloned.1.call-done = f32[8,32,768]{2,1,0:T(8,128)} async-done(((f32[8,128,768]{2,1,0:T(8,128)}), f32[8,32,768]{2,1,0:T(8,128)}) %reduce-scatter.35.cloned.1.call-update) | async-done | bytes 786448 | tf_op jit(solution)/shard_map/reduce_scatter | solution.py:62
  1291.5 68.0 %collective-permute-done.1 = f32[2,8,32,768]{3,2,1,0:T(8,128)} collective-permute-done((f32[2,8,32,768]{3,2,1,0:T(8,128)S(1)}, f32[2,8,32,768]{3,2,1,0:T(8,128)}, u32[]{:S(2)}, u32[]{:S(2)}) %collective-permute-start.1) | collective-permute-done | bytes 1572896 | tf_op jit(solution)/shard_map/ppermute | solution.py:25
  1364.0 18.7 %all-reduce.2 = (f32[768]{0:T(1024)S(1)}, f32[768]{0:T(1024)S(1)}, f32[768]{0:T(1024)S(1)}, f32[768]{0:T(1024)S(1)}, f32[2,768]{1,0:T(2,128)S(1)}, /*index=5*/f3...) all-reduce(f32[768]{0:T(1024)S(1)} %copy-done.52, ...), channel_id=1, replica_groups=mesh['ctx'=8,'tp'=4] {'tp'}, use_global_device_ids=true, to_apply=%region_48.49 | all-reduce | flops 9216 | bytes 73728 | tf_op jit(solution)/shard_map/psum | solution.py:266
  1382.8 23.3 %all-reduce = (f32[1,3,2,64]{3,2,1,0:T(2,128)S(1)}, f32[1,3,2,64]{3,2,1,0:T(2,128)S(1)}, f32[1,768]{1,0:T(1,128)S(1)}, f32[1,768]{1,0:T(1,128)S(1)}, f32[1,768]{...) all-reduce(f32[1,3,2,64]{3,2,1,0:T(2,128)S(1)} %maximum_bitcast_fus, ...), channel_id=1, replica_groups=mesh['ctx'=8,'tp'=4] {'ctx'}, use_global_device_ids=true, to_apply=%region_41.42 | all-reduce | flops 11520 | bytes 92160 | tf_op jit(solution)/shard_map/psum | solution.py:291
  1409.8 74.9 %all-reduce.5.cloned.1.call-done = (f32[1,768,3,3,64]{1,4,3,2,0:T(8,128)}, f32[1,768,3,3,64]{1,4,3,2,0:T(8,128)}, f32[1,192,768]{2,1,0:T(8,128)}, f32[1,192,768]...) async-done(((f32[1,768,3,3,64]{1,4,3,2,0:T(8,128)}, f32[1,768,3,3,64]{1,4,3,2,0:T(8,128)}, ...) | async-done | bytes 14155792 | tf_op jit(solution)/shard_map/psum | solution.py:291
  1497.6 52.9 %all-gather.35.cloned.1.call-done = f32[8,128,768]{2,1,0:T(8,128)} async-done(((f32[8,32,768]{2,1,0:T(8,128)}), f32[8,128,768]{2,1,0:T(8,128)}) %all-gather.35.cloned.1.call-update) | async-done | bytes 3145744 | tf_op jit(solution)/shard_map/all_gather | solution.py:365
  (384 shorter events, 238.2 us)
Async XLA Ops:
  7.2 39.4 %all-gather.15.cloned.1.call-start = ((), (), s32[]{:S(2)}) async-start(), calls=%async_computation.13 | async-start | bytes 3538944 | tf_op jit(solution)/shard_map/all_gather | solution.py:102
  10.9 71.0 %all-gather.13.cloned.1.call-start = ((), (), s32[]{:S(2)}) async-start(), calls=%async_computation.12 | async-start | bytes 3538944 | tf_op jit(solution)/shard_map/all_gather | solution.py:103
  12.1 141.8 %reduce-scatter.13.cloned.1.call-start = ((), (), s32[]{:S(2)}) async-start(), calls=%async_computation.14 | async-start | bytes 3932160 | tf_op jit(solution)/shard_map/reduce_scatter | solution.py:62
  93.5 100.3 %all-gather.17.cloned.1.call-start = ((), (), s32[]{:S(2)}) async-start(), calls=%async_computation.15 | async-start | bytes 1966080 | tf_op jit(solution)/shard_map/all_gather | solution.py:66
  93.7 168.2 %copy-start.32 = (f32[768]{0:T(1024)}, f32[768]{0:T(1024)S(1)}, u32[]{:S(2)}) copy-start(f32[768]{0:T(1024)S(1)} %get-tuple-element.126) | copy-start | bytes 9220
  93.7 351.5 %copy-start.34 = (f32[768]{0:T(1024)}, f32[768]{0:T(1024)S(1)}, u32[]{:S(2)}) copy-start(f32[768]{0:T(1024)S(1)} %get-tuple-element.127) | copy-start | bytes 9220
  155.6 106.3 %copy-start.36 = (f32[8,32]{1,0:T(8,128)}, f32[8,32]{1,0:T(8,128)S(1)}, u32[]{:S(2)}) copy-start(f32[8,32]{1,0:T(8,128)S(1)} %fusion.87) | copy-start | bytes 3076
  156.6 105.3 %reduce-scatter.15.cloned.1.call-start = ((), (), s32[]{:S(2)}) async-start(), calls=%async_computation.16 | async-start | bytes 3932160 | tf_op jit(solution)/shard_map/reduce_scatter | solution.py:62
  156.7 439.4 %copy-start.69 = (f32[768]{0:T(1024)}, f32[768]{0:T(1024)S(1)}, u32[]{:S(2)}) copy-start(f32[768]{0:T(1024)S(1)} %get-tuple-element.36) | copy-start | bytes 9220
  202.6 99.3 %all-gather.19.cloned.1.call-start = ((), (), s32[]{:S(2)}) async-start(), calls=%async_computation.17 | async-start | bytes 1966080 | tf_op jit(solution)/shard_map/all_gather | solution.py:66
  263.7 181.5 %copy-start.38 = (f32[8,32]{1,0:T(8,128)}, f32[8,32]{1,0:T(8,128)S(1)}, u32[]{:S(2)}) copy-start(f32[8,32]{1,0:T(8,128)S(1)} %fusion.88) | copy-start | bytes 3076
  264.7 74.1 %all-gather.23.cloned.1.call-start = ((), (), s32[]{:S(2)}) async-start(), calls=%async_computation.19 | async-start | bytes 3538944 | tf_op jit(solution)/shard_map/all_gather | solution.py:102
  306.9 67.1 %all-gather.21.cloned.1.call-start = ((), (), s32[]{:S(2)}) async-start(), calls=%async_computation.18 | async-start | bytes 3538944 | tf_op jit(solution)/shard_map/all_gather | solution.py:103
  309.2 136.0 %reduce-scatter.17.cloned.1.call-start = ((), (), s32[]{:S(2)}) async-start(), calls=%async_computation.20 | async-start | bytes 3932160 | tf_op jit(solution)/shard_map/reduce_scatter | solution.py:62
  384.8 100.4 %all-gather.25.cloned.1.call-start = ((), (), s32[]{:S(2)}) async-start(), calls=%async_computation.21 | async-start | bytes 1966080 | tf_op jit(solution)/shard_map/all_gather | solution.py:66
  448.0 105.3 %reduce-scatter.19.cloned.1.call-start = ((), (), s32[]{:S(2)}) async-start(), calls=%async_computation.22 | async-start | bytes 3932160 | tf_op jit(solution)/shard_map/reduce_scatter | solution.py:62
  494.0 102.0 %all-gather.27.cloned.1.call-start = ((), (), s32[]{:S(2)}) async-start(), calls=%async_computation.23 | async-start | bytes 1966080 | tf_op jit(solution)/shard_map/all_gather | solution.py:66
  558.8 107.8 %reduce-scatter.21.cloned.1.call-start = ((), (), s32[]{:S(2)}) async-start(), calls=%async_computation.24 | async-start | bytes 3932160 | tf_op jit(solution)/shard_map/reduce_scatter | solution.py:62
  607.3 100.9 %all-gather.29.cloned.1.call-start = ((), (), s32[]{:S(2)}) async-start(), calls=%async_computation.25 | async-start | bytes 1966080 | tf_op jit(solution)/shard_map/all_gather | solution.py:66
  670.9 110.5 %reduce-scatter.25.cloned.1.call-start = ((), (), s32[]{:S(2)}) async-start(), calls=%async_computation.27 | async-start | bytes 7077888 | tf_op jit(solution)/shard_map/reduce_scatter | solution.py:233
  720.6 126.2 %reduce-scatter.23.cloned.1.call-start = ((), (), s32[]{:S(2)}) async-start(), calls=%async_computation.26 | async-start | bytes 7077888 | tf_op jit(solution)/shard_map/reduce_scatter | solution.py:230
  742.9 170.0 %reduce-scatter.27.cloned.1.call-start = ((), (), s32[]{:S(2)}) async-start(), calls=%async_computation.28 | async-start | bytes 3932160 | tf_op jit(solution)/shard_map/reduce_scatter | solution.py:62
  852.4 101.1 %all-gather.31.cloned.1.call-start = ((), (), s32[]{:S(2)}) async-start(), calls=%async_computation.29 | async-start | bytes 1966080 | tf_op jit(solution)/shard_map/all_gather | solution.py:66
  916.3 107.8 %reduce-scatter.29.cloned.1.call-start = ((), (), s32[]{:S(2)}) async-start(), calls=%async_computation.30 | async-start | bytes 3932160 | tf_op jit(solution)/shard_map/reduce_scatter | solution.py:62
  964.9 101.5 %all-gather.33.cloned.1.call-start = ((), (), s32[]{:S(2)}) async-start(), calls=%async_computation.31 | async-start | bytes 1966080 | tf_op jit(solution)/shard_map/all_gather | solution.py:66
  1029.1 110.4 %reduce-scatter.33.cloned.1.call-start = ((), (), s32[]{:S(2)}) async-start(), calls=%async_computation.33 | async-start | bytes 7077888 | tf_op jit(solution)/shard_map/reduce_scatter | solution.py:233
  1078.6 126.3 %reduce-scatter.31.cloned.1.call-start = ((), (), s32[]{:S(2)}) async-start(), calls=%async_computation.32 | async-start | bytes 7077888 | tf_op jit(solution)/shard_map/reduce_scatter | solution.py:230
  1103.1 183.4 %reduce-scatter.35.cloned.1.call-start = ((), (), s32[]{:S(2)}) async-start(), calls=%async_computation.34 | async-start | bytes 3932160 | tf_op jit(solution)/shard_map/reduce_scatter | solution.py:62
  1209.5 275.1 %all-reduce.5.cloned.1.call-start = ((), (), s32[]{:S(2)}) async-start(), calls=%async_computation.36 | async-start | bytes 28311552 | tf_op jit(solution)/shard_map/psum | solution.py:291
  1232.4 318.1 %all-gather.35.cloned.1.call-start = ((), (), s32[]{:S(2)}) async-start(), calls=%async_computation.35 | async-start | bytes 3932160 | tf_op jit(solution)/shard_map/all_gather | solution.py:365
  1233.5 55.2 %collective-permute-start = (f32[1,8,32,768]{3,2,1,0:T(8,128)S(1)}, f32[1,8,32,768]{3,2,1,0:T(8,128)S(1)}, u32[]{:S(2)}, u32[]{:S(2)}) collective-permute-start(f32[1,8,32,768]{3,2,1,0:T(8,128)S(1)} %copy-done.13), channel_id=1, source_target_pairs={{0,1},{1,0},{2,3},{3,2},{4,5},{5,4},{6,7},{7,6},{8,9},{9,8},{10,11... | collective-permute-start | bytes 2359304 | tf_op jit(solution)/shard_map/ppermute | solution.py:25
  1289.0 70.6 %collective-permute-start.1 = (f32[2,8,32,768]{3,2,1,0:T(8,128)S(1)}, f32[2,8,32,768]{3,2,1,0:T(8,128)}, u32[]{:S(2)}, u32[]{:S(2)}) collective-permute-start(f32[2,8,32,768]{3,2,1,0:T(8,128)S(1)} %pad_maximum_fusion.3), channel_id=1, source_target_pairs={{0,2},{1,3},{2,0},{3,1},{4,6},{5,7},{6,4},{7,5},{8,10},{9,11},{10,... | collective-permute-start | bytes 4718600 | tf_op jit(solution)/shard_map/ppermute | solution.py:25
  (88 other events, 1388.4 us)
Sparse Core Ops, SparseCore 0:
  11.1 35.5 all-gather.14
  49.1 32.8 all-gather.12
  93.6 60.2 reduce-scatter.12
  156.7 37.1 all-gather.16
  202.7 59.1 reduce-scatter.14
  264.8 37.0 all-gather.18
  307.1 31.6 all-gather.22
  341.2 32.8 all-gather.20
  385.0 60.2 reduce-scatter.16
  448.1 37.1 all-gather.24
  494.2 59.1 reduce-scatter.18
  558.9 37.0 all-gather.26
  607.4 59.0 reduce-scatter.20
  671.1 37.1 all-gather.28
  720.7 60.6 reduce-scatter.24
  785.0 61.7 reduce-scatter.22
  852.6 60.2 reduce-scatter.26
  916.4 37.0 all-gather.30
  965.0 59.0 reduce-scatter.28
  1029.2 37.1 all-gather.32
  1078.8 60.6 reduce-scatter.32
  1143.2 61.7 reduce-scatter.30
  1209.6 76.7 reduce-scatter.34
  1292.2 192.4 all-reduce.4
  1486.9 63.5 all-gather.34
